TPU v7x, 768 devices: a whole 4x8x12 slice. The times are simulated.
768 devices in a mesh: grid: 24 (over y_hi, z), rep: 32 (over x, y_lo, core).
Axes of the slice: x: 4, y: 8 (y_hi: 2, y_lo: 4; y = y_hi * 4 + y_lo), z: 12, core: 2. Of those that a mesh axis runs over, the one named last changes fastest.
Arguments:
- amplitudes: bfloat16 [96, 960, 960], P('grid', 'rep'), may hold values from -6 to 6
- vvvv_panel: bfloat16 [960, 960, 1920], P('rep', 'grid'), may hold values from -0.01171875 to 0.01171875
- fock_window: bfloat16 [960, 2], P('rep'), may hold values from -0.375 to 0.375
- orbital_irrep: int32 [960], replicated, may hold values from 0 to 3, as said below
- pair_irrep: int32 [96], replicated, may hold values from 0 to 3
- virtual_panel: int32 [2], replicated, may hold values from 0 to 959
Outputs:
- residual: float32 [96, 2, 960], P('rep', None, 'grid')
Inputs may be any that keep to these rules, and one draw needn't show every extreme that they name: `orbital_irrep`: the virtual orbitals form four contiguous runs of 240 orbitals each; every orbital of a run has the same irrep, and each irrep 0 to 3 holds exactly one run, in an order that varies from draw to draw.
All inputs are finite; a program needn't handle non-finite values.
Results may differ from a plain program's by a relative error of at most 0.00035.
Values may be sent and summed in bfloat16 or wider, within the bound.
No kernel may reach another device: no remote copies, remote signals or barrier semaphores. Data moves between devices by JAX's collectives and lax.ppermute only.
A program may use at most 64 MiB of HBM per device.

v0:
```python
import jax
import jax.numpy as jnp
from jax import lax
from jax.sharding import PartitionSpec as P


def shards(amplitudes, vvvv_panel, fock_window, orbital_irrep, pair_irrep, virtual_panel):
    pair_local = amplitudes.shape[0]
    virt_local = amplitudes.shape[1]
    full_virt = amplitudes.shape[2]
    col_local = vvvv_panel.shape[1]
    panel_width = vvvv_panel.shape[2] // full_virt
    grid_index = lax.axis_index("grid")
    rep_index = lax.axis_index("rep")
    row_irreps = lax.dynamic_slice_in_dim(orbital_irrep, rep_index * virt_local, virt_local, 0)
    col_irreps = lax.dynamic_slice_in_dim(orbital_irrep, grid_index * col_local, col_local, 0)
    pair_local_irreps = lax.dynamic_slice_in_dim(pair_irrep, grid_index * pair_local, pair_local, 0)
    panel_irrep = orbital_irrep[virtual_panel]
    row_sym = jnp.bitwise_xor(row_irreps[:, None], orbital_irrep[None, :])
    amp_mask = row_sym[None, :, :] == pair_local_irreps[:, None, None]
    masked_amps = jnp.where(amp_mask, amplitudes, jnp.zeros_like(amplitudes))
    target_cols = jnp.bitwise_xor(col_irreps[:, None], panel_irrep[None, :])
    panel_four = vvvv_panel.reshape(virt_local, col_local, panel_width, full_virt)
    w_mask = row_sym[:, None, None, :] == target_cols[None, :, :, None]
    masked_w = jnp.where(w_mask, panel_four, jnp.zeros_like(panel_four))
    fock_mask = row_irreps[:, None] == panel_irrep[None, :]
    masked_f = jnp.where(fock_mask, fock_window, jnp.zeros_like(fock_window))
    col_start = grid_index * col_local
    block_rows = lax.all_gather(masked_amps, "grid", axis=0, tiled=True)
    row_count = block_rows.shape[0]
    ladder = jnp.einsum("ncd,cabd->nba", block_rows, masked_w, preferred_element_type=jnp.float32)
    own_cols = lax.dynamic_slice_in_dim(block_rows, col_start, col_local, 2)
    fock_term = jnp.einsum("pca,cb->pba", own_cols, masked_f, preferred_element_type=jnp.float32)
    partials = (ladder + fock_term).reshape(row_count, panel_width * col_local)
    pair_total = partials.shape[0]
    out_rows = pair_total // lax.axis_size("rep")
    summed = lax.psum_scatter(partials, "rep", scatter_dimension=0, tiled=True)
    return summed.reshape(out_rows, panel_width, col_local)


def solution(mesh):
    return jax.shard_map(
        shards,
        mesh=mesh,
        in_specs=(P("grid", "rep", None), P("rep", "grid", None), P("rep", None), P(), P(), P()),
        out_specs=P("rep", None, "grid"),
        check_vma=False,
    )
```

profile of v0, /device:TPU:1, one launch (start us, length us, event | category | flops | bytes accessed | tf_op | source)
XLA Modules:
  0.0 362.1 jit_solution(6803572842348747029)
XLA Ops:
  6.5 0.0 all-gather.2.cloned.1.call-start
  6.5 0.8 dynamic_slice.12
  7.3 0.8 broadcast_xor_fusion
  8.1 0.7 dynamic_slice.14
  8.8 1.8 compare_select_fusion.6
  10.6 0.0 all-gather.2.cloned.1.call-update
  10.6 0.7 compare_select_fusion.7
  11.3 1.3 gather_fusion
  12.6 0.8 dynamic_slice.13
  13.4 0.0 copy-start
  13.4 13.3 %reshape.85 = bf16[30,40,2,960]{3,2,1,0:T(2,128)(2,1)} reshape(bf16[30,40,1920]{2,1,0:T(8,128)(2,1)} %param.7) | data formatting | bytes 9216000 | tf_op jit(solution)/shard_map/reshape | solution.py:23
  26.6 1.3 dynamic-slice
  28.6 0.1 broadcast_xor_fusion.1
  28.6 176.4 %all-gather.2.cloned.1.call-done = bf16[96,30,960]{2,1,0:T(8,128)(2,1)} async-done(((bf16[4,30,960]{2,1,0:T(8,128)(2,1)}), bf16[96,30,960]{2,1,0:T(8,128)(2,1)}) %all-gather.2.cloned.1.call-update) | async-done | bytes 5529616 | tf_op jit(solution)/shard_map/all_gather | solution.py:29
  205.1 1.7 constant_dynamic-slice_fusion.1
  206.8 1.1 copy.24
  207.9 0.0 copy-done
  207.9 0.2 fusion.14
  208.1 12.7 %fusion.10 = f32[96,2,40]{0,2,1:T(8,128)S(1)} fusion(bf16[96,30,960]{2,1,0:T(8,128)(2,1)} %all-gather.2.cloned.1.call-done, bf16[30,40,2,960]{3,2,1,0:T(2,128)(2,1)} %reshape.85, s32[40,2]{0,1:T(2,128)S(1)} %broadcast_xor_fusion.1, s32[30,960]{1,0:T(8,128)S(1)} %broadcast_xor_fusion, f32[2,96,40]{1,0,2:T(2,128)S(1)} %fusion.14), kind=kOutput, calls=%fused_computation.10 | convolution fusion | flops 446983680 | bytes 10314560 | tf_op jit(solution)/shard_map/ncd,cabd->nba/dot_general | solution.py:31
  220.8 133.7 %all-reduce = f32[96,80]{0,1:T(8,128)S(1)} all-reduce(f32[96,80]{0,1:T(8,128)S(1)} %bitcast.26), channel_id=2, replica_groups=mesh['grid'=24,'rep'=32] {'rep'}, use_global_device_ids=true, to_apply=%region_0.1.clone | all-reduce | flops 7680 | bytes 61440
  354.5 0.1 constant_dynamic-slice_fusion
  354.6 0.7 copy.20
  (1 shorter events, 0.0 us)
Async XLA Ops:
  6.5 198.5 %all-gather.2.cloned.1.call-start = ((), (), s32[]{:S(2)}) async-start(), calls=%async_computation | async-start | bytes 6553600 | tf_op jit(solution)/shard_map/all_gather | solution.py:29
  13.4 194.5 %copy-start = (bf16[30,2]{0,1:T(2,128)(2,1)S(1)}, bf16[30,2]{0,1:T(2,128)(2,1)}, u32[]{:S(2)}) copy-start(bf16[30,2]{0,1:T(2,128)(2,1)} %param.8) | copy-start | bytes 364
Sparse Core Ops, SparseCore 0:
  10.9 194.0 all-gather.1
where the time goes:
time: 365 us; the launch traced here: 362 us
  waiting for transfers between devices  176 us (48%)
  blocking collectives  134 us (37%)
  local copies, waits for them, and re-layouts  21.7 us (6%)
  between operations  14.1 us (4%)
  matrix products  12.9 us (4%)
    all_gather x1, waiting for transfers between devices, shards(): block_rows = lax.all_gather(masked_amps, 'grid', axis=0, tiled=True)  176 us
    unnamed x1, blocking collectives  134 us
    reshape x1, local copies, waits for them, and re-layouts, shards(): vvvv_panel.reshape(virt_local, col_local, panel_width, full_virt)  13.3 us
    dot_general x1, matrix products, shards(): jnp.einsum('ncd,cabd->nba', block_rows, masked_w, preferred_element_type=...  12.7 us
  transfers between devices with their start and end apart: 1, of which 1 were waited for; matrix products, arithmetic and copies ran while one was open for 5% of the time, Pallas kernels for 0%

commit v1 on v0

v1 whole, which is shorter than its diff:
```python
import jax
import jax.numpy as jnp
from jax import lax
from jax.sharding import PartitionSpec as P

RUNS = 4
PLANES = 2


def shards(amplitudes, vvvv_panel, fock_window, orbital_irrep, pair_irrep, virtual_panel):
    pair_local, virt_local, full_virt = amplitudes.shape
    col_local = vvvv_panel.shape[1]
    panel_width = vvvv_panel.shape[2] // full_virt
    run = full_virt // RUNS
    groups = lax.axis_size("grid")
    ring = groups // PLANES
    reps = lax.axis_size("rep")
    grid_index = lax.axis_index("grid")
    rep_index = lax.axis_index("rep")

    run_irrep = orbital_irrep[::run]
    row_irrep = orbital_irrep[rep_index * virt_local]
    col_irrep = orbital_irrep[grid_index * col_local]
    panel_irrep = orbital_irrep[virtual_panel]

    own_pairs = lax.dynamic_slice_in_dim(pair_irrep, grid_index * pair_local, pair_local, 0)
    own_want = jnp.bitwise_xor(own_pairs, row_irrep)
    packed = jnp.zeros((pair_local, virt_local, run), amplitudes.dtype)
    for k in range(RUNS):
        packed = jnp.where(
            (own_want == run_irrep[k])[:, None, None], amplitudes[:, :, k * run : (k + 1) * run], packed
        )

    z_groups = [list(range(h * ring, (h + 1) * ring)) for h in range(PLANES)]
    other = lax.ppermute(packed, "grid", [(g, (g + ring) % groups) for g in range(groups)])
    own_ring = lax.all_to_all(
        jnp.broadcast_to(packed[None], (ring, pair_local, virt_local, run)),
        "grid", 0, 0, tiled=True, axis_index_groups=z_groups,
    ).reshape(ring * pair_local, virt_local, run)
    other_ring = lax.all_gather(other, "grid", axis=0, tiled=True, axis_index_groups=z_groups)

    plane = grid_index // ring
    first = jnp.where(plane == 0, own_ring, other_ring)
    second = jnp.where(plane == 0, other_ring, own_ring)
    rows = jnp.concatenate([first, second], axis=0)

    w_want = jnp.bitwise_xor(jnp.bitwise_xor(row_irrep, col_irrep), panel_irrep)
    ladder = []
    for b in range(panel_width):
        start = jnp.argmax(run_irrep == w_want[b]).astype(jnp.int32) * run + b * full_virt
        w_run = lax.dynamic_slice_in_dim(vvvv_panel, start, run, 2)
        keep = pair_irrep == jnp.bitwise_xor(col_irrep, panel_irrep[b])
        part = jnp.einsum("ncd,cad->na", rows, w_run, preferred_element_type=jnp.float32)
        ladder.append(jnp.where(keep[:, None], part, 0.0))
    ladder = jnp.stack(ladder, axis=1)

    own_cols = lax.dynamic_slice_in_dim(rows, (grid_index * col_local) % run, col_local, 2)
    f_keep = row_irrep == panel_irrep
    masked_f = jnp.where(f_keep[None, :], fock_window, jnp.zeros_like(fock_window))
    fock = jnp.einsum("pca,cb->pba", own_cols, masked_f, preferred_element_type=jnp.float32)
    fock = jnp.where((jnp.bitwise_xor(pair_irrep, row_irrep) == col_irrep)[:, None, None], fock, 0.0)
    partial = ladder + fock

    pairs = partial.shape[0]
    out_rows = pairs // reps
    sent = partial.reshape(reps, out_rows * panel_width * col_local)
    got = lax.all_to_all(sent, "rep", 0, 0, tiled=True)
    return jnp.sum(got, axis=0).reshape(out_rows, panel_width, col_local)


def solution(mesh):
    return jax.shard_map(
        shards,
        mesh=mesh,
        in_specs=(P("grid", "rep", None), P("rep", "grid", None), P("rep", None), P(), P(), P()),
        out_specs=P("rep", None, "grid"),
        check_vma=False,
    )
```

time: 365 us -> 102 us (0.28)
  waiting for transfers between devices: 176 us -> 0.01 us
  blocking collectives: 134 us -> 49.9 us
  starting transfers between devices: 0.01 us -> 23.2 us
  local copies, waits for them, and re-layouts: 21.7 us -> 9.16 us
  matrix products: 12.9 us -> 3.94 us
  between operations: 14.1 us -> 5.17 us
  other arithmetic: 3.29 us -> 9.73 us
    all_gather x1 -> x0, waiting for transfers between devices: 176 us -> none  [shards(): block_rows = lax.all_gather(masked_amps, 'grid', axis=0, tiled=True)]
    unnamed x1 -> x0, blocking collectives: 134 us -> none
    all_gather x0 -> x1, blocking collectives: none -> 32.6 us  [shards(): lax.all_gather(other, 'grid', axis=0, tiled=True, axis_index_groups=z_gro...]
    all_to_all x0 -> x1, blocking collectives: none -> 17.3 us  [shards(): got = lax.all_to_all(sent, 'rep', 0, 0, tiled=True)]
    all_to_all x0 -> x1, starting transfers between devices: none -> 14.9 us  [shards(): lax.all_to_all(jnp.broadcast_to(packed[None], (ring, pair_local, virt_loc...]
    reshape x2, local copies, waits for them, and re-layouts: 13.9 us -> 1.11 us  [the longest x1 0.67 us: shards(): return jnp.sum(got, axis=0).reshape(out_rows, panel_width, col_local)]
    dot_general x1 -> x2, matrix products: 12.7 us -> 3.72 us  [shards(): jnp.einsum('ncd,cad->na', rows, w_run, preferred_element_type=jnp.float32)]
    ppermute x0 -> x1, starting transfers between devices: none -> 8.28 us  [shards(): lax.ppermute(packed, 'grid', [(g, (g + ring) % groups) for g in range(gro...]
  transfers between devices with their start and end apart: 1 -> 2, of which waited for: 1 -> 0; matrix products, arithmetic and copies ran while one was open for 5% -> 7% of each run, Pallas kernels for 0% -> 0%
where the time goes in v1:
time: 102 us; the launch traced here: 101 us
  blocking collectives  49.9 us (49%)
  starting transfers between devices  23.2 us (23%)
  other arithmetic  9.73 us (10%)
  local copies, waits for them, and re-layouts  9.16 us (9%)
  between operations  5.17 us (5%)
  matrix products  3.94 us (4%)
    all_gather x1, blocking collectives, shards(): lax.all_gather(other, 'grid', axis=0, tiled=True, axis_index_groups=z_gro...  32.6 us
    all_to_all x1, blocking collectives, shards(): got = lax.all_to_all(sent, 'rep', 0, 0, tiled=True)  17.3 us
    all_to_all x1, starting transfers between devices, shards(): lax.all_to_all(jnp.broadcast_to(packed[None], (ring, pair_local, virt_loc...  14.9 us
    ppermute x1, starting transfers between devices, shards(): lax.ppermute(packed, 'grid', [(g, (g + ring) % groups) for g in range(gro...  8.28 us
    eq x2, other arithmetic, shards(): own_want == run_irrep[k]  3.94 us
    dot_general x2, matrix products, shards(): jnp.einsum('ncd,cad->na', rows, w_run, preferred_element_type=jnp.float32)  3.72 us
    another operation x2, other arithmetic, shards(): jnp.argmax(run_irrep == w_want[b]).astype(jnp.int32) * run + b * full_virt  2.61 us
  transfers between devices with their start and end apart: 2, of which 0 were waited for; matrix products, arithmetic and copies ran while one was open for 7% of the time, Pallas kernels for 0%

profile of v1, /device:TPU:1, one launch (start us, length us, event | category | flops | bytes accessed | tf_op | source)
XLA Modules:
  0.0 101.1 jit_solution(9866256783093616570)
XLA Ops:
  0.0 1.2 %fusion.18 = (bf16[4,30,240]{2,0,1:T(4,128)(2,1)S(1)}, bf16[4,30,240]{2,0,1:T(4,128)(2,1)S(1)}, bf16[4,30,240]{2,0,1:T(4,128)(2,1)S(1)}, bf16[4,30,240]{2,0,1:T(4,128)(2,1)S(1)}) fusion(bf16[4,30,960]{2,0,1:T(4,128)(2,1)} %param.6), kind=kLoop, calls=%fused_computation.44 | loop fusion | bytes 460800 | tf_op jit(solution)/shard_map/slice | solution.py:31
  1.2 0.8 slice.40
  2.0 0.6 fusion.22
  2.6 1.4 %fusion.19 = (s32[1]{0:T(128)}, s32[1]{0:T(128)}) fusion(s32[960]{0:T(1024)} %param.9, s32[]{:T(128)S(6)} %select_n.81, s32[]{:T(128)S(6)} %select_n.86), kind=kLoop, calls=%fused_computation.45 | loop fusion | bytes 24 | tf_op jit(solution)/shard_map/dynamic_slice | solution.py:23
  4.1 2.0 %broadcast_compare_fusion.5 = (pred[4]{0:T(512)(128)(4,1)S(1)}, s32[4]{0:T(128)S(1)}) fusion(s32[]{:T(128)} %bitcast.3, s32[]{:T(128)} %bitcast.2, s32[96]{0:T(128)} %param.10, s32[]{:T(128)S(6)} %select_n.85), kind=kLoop, calls=%fused_computation.39 | loop fusion | flops 8 | bytes 48 | tf_op jit(solution)/shard_map/eq | solution.py:31
  6.1 1.9 %broadcast_compare_fusion.4 = (pred[4]{0:T(512)(128)(4,1)S(1)}, pred[4]{0:T(512)(128)(4,1)S(1)}, pred[4]{0:T(512)(128)(4,1)S(1)}) fusion(s32[4]{0:T(128)S(1)} %get-tuple-element.10, s32[]{:T(128)} %bitcast.4, s32[]{:T(128)} %bitcast.5, s32[]{:T(128)} %bitcast.6), kind=kLoop, calls=%fused_computation.38 | loop fusion | flops 12 | bytes 40 | tf_op jit(solution)/shard_map/eq | solution.py:31
  8.1 8.3 %collective-permute-start = (bf16[4,30,240]{2,1,0:T(8,128)(2,1)S(1)}, bf16[4,30,240]{2,1,0:T(8,128)(2,1)S(1)}, u32[]{:S(2)}, u32[]{:S(2)}) collective-permute-start(bf16[4,30,240]{2,1,0:T(8,128)(2,1)S(1)} %fusion.9), channel_id=1, source_target_pairs={{0,384},{32,416},{64,448},{96,480},{128,512},{160,544},{192,576},{... | collective-permute-start | bytes 172808 | tf_op jit(solution)/shard_map/ppermute | solution.py:35
  16.4 1.1 %broadcast_in_dim.91 = bf16[12,4,30,240]{3,1,2,0:T(4,128)(2,1)} broadcast(bf16[4,30,240]{2,0,1:T(4,128)(2,1)S(1)} %copy.16), dimensions={1,2,3} | broadcast | bytes 748800 | tf_op jit(solution)/shard_map/broadcast_in_dim | solution.py:37
  17.5 14.9 %all-to-all-start = ((bf16[12,4,30,240]{3,1,2,0:T(4,128)(2,1)}), bf16[12,4,30,240]{3,1,2,0:T(4,128)(2,1)S(1)}, u32[]{:S(2)}, u32[]{:S(2)}) async-start(bf16[12,4,30,240]{3,1,2,0:T(4,128)(2,1)} %broadcast_in_dim.91), calls=%async_computation | async-start | bytes 1474560 | tf_op jit(solution)/shard_map/all_to_all | solution.py:36
  32.4 0.6 gather_fusion
  34.4 0.6 fusion.20
  37.4 0.6 fusion.21
  38.0 1.3 %compare_reduce_fusion = (pred[]{:T(512)}, s32[]{:T(128)}) fusion(s32[4]{0:T(128)S(1)} %slice.40, s32[]{:T(128)} %bitcast.11), kind=kLoop, calls=%fused_computation.23 | loop fusion | flops 25 | bytes 25 | tf_op jit(solution)/shard_map/shards/reduce | solution.py:50
  39.3 1.4 %compare_reduce_fusion.1 = (pred[]{:T(512)}, s32[]{:T(128)}) fusion(s32[4]{0:T(128)S(1)} %slice.40, s32[]{:T(128)} %bitcast.7), kind=kLoop, calls=%fused_computation.24 | loop fusion | flops 25 | bytes 25 | tf_op jit(solution)/shard_map/shards/reduce | solution.py:50
  40.6 1.3 %xor_compare_fusion = (pred[96]{0:T(512)(128)(4,1)S(1)}, pred[96]{0:T(512)(128)(4,1)S(1)}, pred[96]{0:T(512)(128)(4,1)S(1)}) fusion(s32[96]{0:T(128)S(1)} %copy-done.1, s32[]{:T(128)} %bitcast, s32[]{:T(128)} %bitcast.2, s32[]{:T(128)S(6)} %xor.27, s32[]{:T(128)S(6)} %xor.33), kind=kLoop, calls=%fused_computation.30 | loop fusion | flops 384 | bytes 688 | tf_op jit(solution)/shard_map/eq | solution.py:61
  41.9 0.7 broadcast_compare_fusion
  43.9 32.6 %all_gather.3 = bf16[48,30,240]{2,1,0:T(8,128)(2,1)S(1)} all-gather(bf16[4,30,240]{2,1,0:T(8,128)(2,1)S(1)} %collective-permute-done), channel_id=1, replica_groups={{0,32,64,96,128,160,192,224,256,288,320,352},{384,416,448,480,512,544,5..., dimensions={0}, use_global_device_ids=true | all-gather | bytes 748800 | tf_op jit(solution)/shard_map/all_gather | solution.py:40
  77.2 0.5 broadcast_select_fusion.1
  77.6 0.6 fusion.4
  78.2 0.6 copy.20
  78.8 1.9 %fusion.1 = f32[96,1,40]{0,2,1:T(8,128)S(1)} fusion(bf16[48,30,240]{2,0,1:T(8,128)(2,1)S(1)} %get-tuple-element.12, bf16[48,30,240]{2,0,1:T(8,128)(2,1)S(1)} %get-tuple-element.11, bf16[30,40,1920]{2,1,0:T(8,128)(2,1)} %param.7, s32[]{:T(128)S(6)} %select_n.95, pred[96]{0:T(512)(128)(4,1)S(1)} %get-tuple-element.21), kind=kOutput, calls=%fused_computation.6 | convolution fusion | flops 58064640 | bytes 2012260 | tf_op jit(solution)/shard_map/ncd,cad->na/dot_general | solution.py:53
  80.6 1.9 %fusion.3 = f32[96,1,40]{0,2,1:T(8,128)S(1)} fusion(bf16[48,30,240]{2,0,1:T(8,128)(2,1)S(1)} %get-tuple-element.12, bf16[48,30,240]{2,0,1:T(8,128)(2,1)S(1)} %get-tuple-element.11, bf16[30,40,1920]{2,1,0:T(8,128)(2,1)} %param.7, s32[]{:T(128)S(6)} %select_n.93, pred[96]{0:T(512)(128)(4,1)S(1)} %get-tuple-element.20), kind=kOutput, calls=%fused_computation.9 | convolution fusion | flops 58064640 | bytes 2012260 | tf_op jit(solution)/shard_map/ncd,cad->na/dot_general | solution.py:53
  83.0 17.3 %all_to_all.15 = f32[32,1,240]{2,1,0:T(1,128)S(1)} all-to-all(f32[32,1,240]{2,1,0:T(1,128)S(1)} %all_to_all.12), channel_id=1, replica_groups=mesh['grid'=24,'rep'=32] {'rep'}, dimensions={0} | all-to-all | bytes 61440 | tf_op jit(solution)/shard_map/all_to_all | solution.py:67
  100.4 0.7 reshape.22
  (22 shorter events, 1.4 us)
Async XLA Ops:
  1.2 31.2 %copy-start.3 = (s32[2]{0:T(128)S(1)}, s32[2]{0:T(128)}, u32[]{:S(2)}) copy-start(s32[2]{0:T(128)} %param.11) | copy-start | bytes 28
  1.2 31.3 %copy-start = (s32[960]{0:T(1024)S(1)}, s32[960]{0:T(1024)}, u32[]{:S(2)}) copy-start(s32[960]{0:T(1024)} %param.9) | copy-start | bytes 11524
  8.1 32.5 %copy-start.1 = (s32[96]{0:T(128)S(1)}, s32[96]{0:T(128)}, u32[]{:S(2)}) copy-start(s32[96]{0:T(128)} %param.10) | copy-start | bytes 1156
  8.1 35.8 %collective-permute-start = (bf16[4,30,240]{2,1,0:T(8,128)(2,1)S(1)}, bf16[4,30,240]{2,1,0:T(8,128)(2,1)S(1)}, u32[]{:S(2)}, u32[]{:S(2)}) collective-permute-start(bf16[4,30,240]{2,1,0:T(8,128)(2,1)S(1)} %fusion.9), channel_id=1, source_target_pairs={{0,384},{32,416},{64,448},{96,480},{128,512},{160,544},{192,576},{... | collective-permute-start | bytes 172808 | tf_op jit(solution)/shard_map/ppermute | solution.py:35
  17.5 58.9 %all-to-all-start = ((bf16[12,4,30,240]{3,1,2,0:T(4,128)(2,1)}), bf16[12,4,30,240]{3,1,2,0:T(4,128)(2,1)S(1)}, u32[]{:S(2)}, u32[]{:S(2)}) async-start(bf16[12,4,30,240]{3,1,2,0:T(4,128)(2,1)} %broadcast_in_dim.91), calls=%async_computation | async-start | bytes 1474560 | tf_op jit(solution)/shard_map/all_to_all | solution.py:36
  80.6 1.9 %copy-start.2 = (bf16[30,2]{0,1:T(2,128)(2,1)S(1)}, bf16[30,2]{0,1:T(2,128)(2,1)}, u32[]{:S(2)}) copy-start(bf16[30,2]{0,1:T(2,128)(2,1)} %param.8) | copy-start | bytes 364

commit v2 on v0

v2 whole, which is shorter than its diff:
```python
import functools

import jax
import jax.numpy as jnp
from jax import lax
from jax.experimental import pallas as pl
from jax.experimental.pallas import tpu as pltpu
from jax.sharding import PartitionSpec as P

RUNS = 4
SIDES = 2
LANES = 128


def pack_kernel(run, orbital_ref, pair_ref, amps_ref, out_ref, held, sem):
    virt_local, pair_local, _ = amps_ref.shape
    row_irrep = orbital_ref[lax.axis_index("rep") * virt_local]
    first_pair = lax.axis_index("grid") * pair_local
    pair_row = lax.broadcasted_iota(jnp.int32, (1, pair_local, run), 1)
    want = jnp.zeros((1, pair_local, run), jnp.int32)
    for p in range(pair_local):
        want = jnp.where(pair_row == p, pair_ref[first_pair + p] ^ row_irrep, want)
    rows = amps_ref[...].astype(jnp.float32)
    best = rows[:, :, :run]
    for k in range(1, RUNS):
        best = jnp.where(want == orbital_ref[k * run], rows[:, :, k * run : (k + 1) * run], best)
    held[...] = best.astype(held.dtype).reshape(held.shape)
    copies = [pltpu.make_async_copy(held, out_ref.at[i], sem.at[i]) for i in range(out_ref.shape[0])]
    for copy in copies:
        copy.start()
    for copy in copies:
        copy.wait()


def panel_kernel(run, width, own, orbital_ref, panel_ref, w_ref, out_ref, held, sem):
    half, cols, span = held.shape[1:]
    grid_index, rep_index = lax.axis_index("grid"), lax.axis_index("rep")
    side = lax.rem(grid_index, SIDES)
    first = (side if own else 1 - side) * half
    row_irrep = orbital_ref[rep_index * (half * SIDES)]
    col_irrep = orbital_ref[grid_index * cols]
    full = run * RUNS
    copies, shifts = [], []
    for b in range(width):
        want = row_irrep ^ col_irrep ^ orbital_ref[panel_ref[b]]
        start = jnp.int32(0)
        for k in range(1, RUNS):
            start = jnp.where(orbital_ref[k * run] == want, k * run, start)
        start = start + b * full
        tile = jnp.minimum(start // LANES, (width * full - span) // LANES)
        lane = pl.multiple_of(tile * LANES, LANES)
        shifts.append(start - lane)
        copies.append(
            pltpu.make_async_copy(w_ref.at[pl.ds(first, half), :, pl.ds(lane, span)], held.at[b], sem.at[b])
        )
        copies[b].start()
    at = lax.broadcasted_iota(jnp.int32, (span, run), 0) - lax.broadcasted_iota(jnp.int32, (span, run), 1)
    for b in range(width):
        pick = jnp.where(at == shifts[b], 1.0, 0.0).astype(jnp.bfloat16)
        copies[b].wait()
        block = held[b].astype(jnp.float32).reshape(half * cols, span).astype(jnp.bfloat16)
        moved = jnp.dot(block, pick, preferred_element_type=jnp.float32)
        out_ref[:, b * cols : (b + 1) * cols, :] = moved.reshape(half, cols, run).astype(out_ref.dtype)


def shards(amplitudes, vvvv_panel, fock_window, orbital_irrep, pair_irrep, virtual_panel):
    pair_local, virt_local, full_virt = amplitudes.shape
    col_local = vvvv_panel.shape[1]
    panel_width = vvvv_panel.shape[2] // full_virt
    run = full_virt // RUNS
    groups = lax.axis_size("grid")
    reps = lax.axis_size("rep")
    half = virt_local // SIDES
    span = LANES * (-(-(run + LANES - 1) // LANES))
    dtype = amplitudes.dtype
    grid_index = lax.axis_index("grid")
    rep_index = lax.axis_index("rep")
    side = grid_index % SIDES

    smem = pl.BlockSpec(memory_space=pltpu.SMEM)
    vmem = pl.BlockSpec(memory_space=pltpu.VMEM)
    anywhere = pl.BlockSpec(memory_space=pl.ANY)
    copies = groups // SIDES
    sent = pl.pallas_call(
        functools.partial(pack_kernel, run),
        out_shape=jax.ShapeDtypeStruct((copies, SIDES, half, pair_local, run), dtype),
        in_specs=[smem, smem, vmem],
        out_specs=anywhere,
        scratch_shapes=[pltpu.VMEM((SIDES, half, pair_local, run), dtype), pltpu.SemaphoreType.DMA((copies,))],
    )(orbital_irrep, pair_irrep, amplitudes.transpose(1, 0, 2))
    rows = lax.all_to_all(sent.reshape(groups, half, pair_local, run), "grid", 0, 0, tiled=True)

    def window(own):
        return pl.pallas_call(
            functools.partial(panel_kernel, run, panel_width, own),
            out_shape=jax.ShapeDtypeStruct((half, panel_width * col_local, run), dtype),
            in_specs=[smem, smem, anywhere],
            out_specs=vmem,
            scratch_shapes=[
                pltpu.VMEM((panel_width, half, col_local, span), dtype),
                pltpu.SemaphoreType.DMA((panel_width,)),
            ],
            compiler_params=pltpu.CompilerParams(vmem_limit_bytes=32 * 1024 * 1024),
        )(orbital_irrep, virtual_panel, vvvv_panel)

    other = lax.ppermute(window(False), "grid", [(g, g ^ 1) for g in range(groups)])
    kept = window(True)

    row_irrep = orbital_irrep[rep_index * virt_local]
    col_irrep = orbital_irrep[grid_index * col_local]
    panel_irrep = orbital_irrep[virtual_panel]
    own_fock = lax.dynamic_slice_in_dim(fock_window, side * half, half, 0)
    own_fock = jnp.where((row_irrep == panel_irrep)[None, :], own_fock, jnp.zeros_like(own_fock))

    def fock_cols(which):
        col = (which * col_local) % run + jnp.arange(col_local)
        hit = col[None, None, :, None] == jnp.arange(run)
        picked = jnp.where(hit, own_fock[:, :, None, None], jnp.zeros((), dtype))
        return picked.reshape(half, panel_width * col_local, run)

    def product(cols, which):
        left = jnp.einsum("gcjd,cxd->gjx", rows, cols, preferred_element_type=jnp.float32)
        right = jnp.einsum("gcjd,cxd->gjx", rows, fock_cols(which), preferred_element_type=jnp.float32)
        return (left + right).reshape(-1, panel_width * col_local)

    own_part = product(kept, grid_index)
    other_part = product(other, grid_index + 1 - 2 * side)
    partial = jnp.stack([jnp.where(side == 0, own_part, other_part), jnp.where(side == 0, other_part, own_part)])
    keep = pair_irrep[:, None] == jnp.bitwise_xor(col_irrep, panel_irrep)[None, :]
    partial = jnp.where(jnp.repeat(keep, col_local, axis=1)[None], partial, 0.0)

    out_rows = partial.shape[1] // reps
    outgoing = partial.reshape(SIDES * reps, out_rows * panel_width * col_local)
    teams = [
        [(first + s) * reps + r for s in range(SIDES) for r in range(reps)]
        for first in range(0, groups, SIDES)
    ]
    got = lax.all_to_all(outgoing, ("grid", "rep"), 0, 0, tiled=True, axis_index_groups=teams)
    return jnp.sum(got, axis=0).reshape(out_rows, panel_width, col_local)


def solution(mesh):
    return jax.shard_map(
        shards,
        mesh=mesh,
        in_specs=(P("grid", "rep", None), P("rep", "grid", None), P("rep", None), P(), P(), P()),
        out_specs=P("rep", None, "grid"),
        check_vma=False,
    )
```

time: 365 us -> 78.5 us (0.22)
  waiting for transfers between devices: 176 us -> 21.1 us
  blocking collectives: 134 us -> 15 us
  starting transfers between devices: 0.01 us -> 24.4 us
  between operations: 14.1 us -> 0.31 us
  local copies, waits for them, and re-layouts: 21.7 us -> 8.46 us
  matrix products: 12.9 us -> 1.57 us
  Pallas kernels: 0 us -> 5.61 us
    all_gather x1 -> x0, waiting for transfers between devices: 176 us -> none  [shards(): block_rows = lax.all_gather(masked_amps, 'grid', axis=0, tiled=True)]
    unnamed x1 -> x0, blocking collectives: 134 us -> none
    all_to_all x0 -> x1, starting transfers between devices: none -> 21.2 us  [shards(): lax.all_to_all(sent.reshape(groups, half, pair_local, run), 'grid', 0, 0,...]
    all_to_all x0 -> x1, blocking collectives: none -> 15 us  [shards(): lax.all_to_all(outgoing, ('grid', 'rep'), 0, 0, tiled=True, axis_index_gr...]
    all_to_all x0 -> x1, waiting for transfers between devices: none -> 14.9 us  [shards(): lax.all_to_all(sent.reshape(groups, half, pair_local, run), 'grid', 0, 0,...]
    reshape x2 -> x1, local copies, waits for them, and re-layouts: 13.9 us -> 0.67 us  [shards(): return jnp.sum(got, axis=0).reshape(out_rows, panel_width, col_local)]
    dot_general x2 -> x4, matrix products: 12.9 us -> 1.57 us  [the longest x2 0.85 us: product(): jnp.einsum('gcjd,cxd->gjx', rows, fock_cols(which), preferred_element_typ...]
    ppermute x0 -> x1, waiting for transfers between devices: none -> 6.22 us  [shards(): lax.ppermute(window(False), 'grid', [(g, g ^ 1) for g in range(groups)])]
  transfers between devices with their start and end apart: 1 -> 2, of which waited for: 1 -> 2; matrix products, arithmetic and copies ran while one was open for 5% -> 6% of each run, Pallas kernels for 0% -> 4%
where the time goes in v2:
time: 78.5 us; the launch traced here: 78.1 us
  starting transfers between devices  24.4 us (31%)
  waiting for transfers between devices  21.1 us (27%)
  blocking collectives  15 us (19%)
  local copies, waits for them, and re-layouts  8.46 us (11%)
  Pallas kernels  5.61 us (7%)
  other arithmetic  1.69 us (2%)
  matrix products  1.57 us (2%)
    all_to_all x1, starting transfers between devices, shards(): lax.all_to_all(sent.reshape(groups, half, pair_local, run), 'grid', 0, 0,...  21.2 us
    all_to_all x1, blocking collectives, shards(): lax.all_to_all(outgoing, ('grid', 'rep'), 0, 0, tiled=True, axis_index_gr...  15 us
    all_to_all x1, waiting for transfers between devices, shards(): lax.all_to_all(sent.reshape(groups, half, pair_local, run), 'grid', 0, 0,...  14.9 us
    ppermute x1, waiting for transfers between devices, shards(): lax.ppermute(window(False), 'grid', [(g, g ^ 1) for g in range(groups)])  6.22 us
    unnamed x16, local copies, waits for them, and re-layouts  5.96 us
    pallas_call x2, Pallas kernels, window(): pl.pallas_call(functools.partial(panel_kernel, run, panel_width, own), ou...  3.44 us
    ppermute x1, starting transfers between devices, shards(): lax.ppermute(window(False), 'grid', [(g, g ^ 1) for g in range(groups)])  3.19 us
    pallas_call x1, Pallas kernels, shards(): pl.pallas_call(functools.partial(pack_kernel, run), out_shape=jax.ShapeDt...  2.18 us
  transfers between devices with their start and end apart: 2, of which 2 were waited for; matrix products, arithmetic and copies ran while one was open for 6% of the time, Pallas kernels for 4%

profile of v2, /device:TPU:1, one launch (start us, length us, event | category | flops | bytes accessed | tf_op | source)
XLA Modules:
  0.0 78.1 jit_solution(1453081617820228624)
XLA Ops:
  0.0 2.2 %shard_map.64 = bf16[12,2,15,4,240]{4,3,2,1,0:T(4,128)(2,1)} custom-call(s32[960]{0:T(1024)} %orbital_ref.5, s32[96]{0:T(128)} %pair_ref.1, bf16[30,4,960]{2,1,0:T(4,128)(2,1)} %bitcast.40), custom_call_target="tpu_custom_call" | custom-call | tf_op jit(solution)/shard_map/pallas_call | solution.py:84
  2.2 21.2 %all-to-all-start = ((bf16[24,15,4,240]{3,2,1,0:T(4,128)(2,1)}), bf16[24,15,4,240]{3,2,1,0:T(4,128)(2,1)S(1)}, u32[]{:S(2)}, u32[]{:S(2)}) async-start(bf16[24,15,4,240]{3,2,1,0:T(4,128)(2,1)} %bitcast.39), calls=%async_computation | async-start | bytes 1474560 | tf_op jit(solution)/shard_map/all_to_all | solution.py:91
  23.4 0.7 copy-done
  24.1 2.3 %copy-done.2 = bf16[30,40,1920]{2,1,0:T(8,128)(2,1)S(1)} copy-done((bf16[30,40,1920]{2,1,0:T(8,128)(2,1)S(1)}, bf16[30,40,1920]{2,1,0:T(8,128)(2,1)}, u32[]{:S(2)}) %copy-start.2) | copy-done | bytes 4608024
  26.4 0.7 copy-done.4
  27.0 1.7 %shard_map.66 = bf16[15,80,240]{2,1,0:T(8,128)(2,1)S(1)} custom-call(s32[960]{0:T(1024)S(1)} %copy-done, s32[2]{0:T(128)S(1)} %copy-done.4, bf16[30,40,1920]{2,1,0:T(8,128)(2,1)S(1)} %copy-done.2), custom_call_target="tpu_custom_call" | custom-call | tf_op jit(solution)/shard_map/pallas_call | solution.py:94
  28.8 3.2 %collective-permute-start = (bf16[15,80,240]{2,1,0:T(8,128)(2,1)S(1)}, bf16[15,80,240]{2,1,0:T(8,128)(2,1)S(1)}, u32[]{:S(2)}, u32[]{:S(2)}) collective-permute-start(bf16[15,80,240]{2,1,0:T(8,128)(2,1)S(1)} %shard_map.66), channel_id=1, source_target_pairs={{0,32},{32,0},{64,96},{96,64},{128,160},{160,128},{192,224},{224,1... | collective-permute-start | bytes 1728008 | tf_op jit(solution)/shard_map/ppermute | solution.py:106
  32.0 2.3 %copy-done.3 = bf16[30,40,1920]{2,1,0:T(8,128)(2,1)S(1)} copy-done((bf16[30,40,1920]{2,1,0:T(8,128)(2,1)S(1)}, bf16[30,40,1920]{2,1,0:T(8,128)(2,1)}, u32[]{:S(2)}) %copy-start.3) | copy-done | bytes 4608024
  34.3 1.7 %shard_map.65 = bf16[15,80,240]{2,1,0:T(8,128)(2,1)S(1)} custom-call(s32[960]{0:T(1024)S(1)} %copy-done.1, s32[2]{0:T(128)S(1)} %copy-done.5, bf16[30,40,1920]{2,1,0:T(8,128)(2,1)S(1)} %copy-done.3), custom_call_target="tpu_custom_call" | custom-call | tf_op jit(solution)/shard_map/pallas_call | solution.py:94
  36.1 0.6 gather_fusion
  36.8 0.6 fusion.20
  37.4 0.6 broadcast_compare_fusion.1
  38.1 0.1 copy.26
  38.4 0.7 broadcast_xor_fusion
  39.1 0.1 copy.24
  39.4 14.9 %all-to-all-done = bf16[24,15,4,240]{3,2,1,0:T(4,128)(2,1)S(1)} async-done(((bf16[24,15,4,240]{3,2,1,0:T(4,128)(2,1)}), bf16[24,15,4,240]{3,2,1,0:T(4,128)(2,1)S(1)}, u32[]{:S(2)}, u32[]{:S(2)}) %all-to-all-start) | async-done | bytes 691232 | tf_op jit(solution)/shard_map/all_to_all | solution.py:91
  54.3 0.4 convolution_bitcast_fusion.2
  54.8 0.4 convolution_bitcast_fusion
  55.2 0.4 fusion
  55.6 6.2 %collective-permute-done = bf16[15,80,240]{2,1,0:T(8,128)(2,1)S(1)} collective-permute-done((bf16[15,80,240]{2,1,0:T(8,128)(2,1)S(1)}, bf16[15,80,240]{2,1,0:T(8,128)(2,1)S(1)}, u32[]{:S(2)}, u32[]{:S(2)}) %collective-permute-start) | collective-permute-done | bytes 576032 | tf_op jit(solution)/shard_map/ppermute | solution.py:106
  61.8 0.4 broadcast_select_fusion.1
  62.2 0.1 select_n.104
  62.4 15.0 %all_to_all.11 = f32[64,1,240]{2,1,0:T(1,128)S(1)} all-to-all(f32[64,1,240]{2,1,0:T(1,128)S(1)} %select_n.104), channel_id=1, replica_groups={{0,1,2,3,4,5,6,7,8,9,10,11,12,13,14,15,16,17,18,19,20,21,22,23,24,25,26..., dimensions={0} | all-to-all | bytes 122880 | tf_op jit(solution)/shard_map/all_to_all | solution.py:138
  77.4 0.7 reshape.140
  (29 shorter events, 0.7 us)
Async XLA Ops:
  0.0 32.0 %copy-start.1 = (s32[960]{0:T(1024)S(1)}, s32[960]{0:T(1024)}, u32[]{:S(2)}) copy-start(s32[960]{0:T(1024)} %orbital_ref.5) | copy-start | bytes 11524
  0.0 32.0 %copy-start.5 = (s32[2]{0:T(128)S(1)}, s32[2]{0:T(128)}, u32[]{:S(2)}) copy-start(s32[2]{0:T(128)} %panel_ref.3) | copy-start | bytes 28
  2.2 52.1 %all-to-all-start = ((bf16[24,15,4,240]{3,2,1,0:T(4,128)(2,1)}), bf16[24,15,4,240]{3,2,1,0:T(4,128)(2,1)S(1)}, u32[]{:S(2)}, u32[]{:S(2)}) async-start(bf16[24,15,4,240]{3,2,1,0:T(4,128)(2,1)} %bitcast.39), calls=%async_computation | async-start | bytes 1474560 | tf_op jit(solution)/shard_map/all_to_all | solution.py:91
  23.4 0.7 copy-start
  24.1 2.3 %copy-start.2 = (bf16[30,40,1920]{2,1,0:T(8,128)(2,1)S(1)}, bf16[30,40,1920]{2,1,0:T(8,128)(2,1)}, u32[]{:S(2)}) copy-start(bf16[30,40,1920]{2,1,0:T(8,128)(2,1)} %w_ref.3) | copy-start | bytes 13824004
  26.4 0.7 copy-start.4
  27.0 10.9 %copy-start.7 = (bf16[30,2]{0,1:T(2,128)(2,1)S(1)}, bf16[30,2]{0,1:T(2,128)(2,1)}, u32[]{:S(2)}) copy-start(bf16[30,2]{0,1:T(2,128)(2,1)} %param.8) | copy-start | bytes 364
  27.0 12.0 %copy-start.6 = (s32[96]{0:T(128)S(1)}, s32[96]{0:T(128)}, u32[]{:S(2)}) copy-start(s32[96]{0:T(128)} %pair_ref.1) | copy-start | bytes 1156
  28.8 33.0 %collective-permute-start = (bf16[15,80,240]{2,1,0:T(8,128)(2,1)S(1)}, bf16[15,80,240]{2,1,0:T(8,128)(2,1)S(1)}, u32[]{:S(2)}, u32[]{:S(2)}) collective-permute-start(bf16[15,80,240]{2,1,0:T(8,128)(2,1)S(1)} %shard_map.66), channel_id=1, source_target_pairs={{0,32},{32,0},{64,96},{96,64},{128,160},{160,128},{192,224},{224,1... | collective-permute-start | bytes 1728008 | tf_op jit(solution)/shard_map/ppermute | solution.py:106
  32.0 2.3 %copy-start.3 = (bf16[30,40,1920]{2,1,0:T(8,128)(2,1)S(1)}, bf16[30,40,1920]{2,1,0:T(8,128)(2,1)}, u32[]{:S(2)}) copy-start(bf16[30,40,1920]{2,1,0:T(8,128)(2,1)} %w_ref.3) | copy-start | bytes 13824004

commit v3 on v2

--- a/solution.py
+++ b/solution.py
@@ -100,10 +100,14 @@
                 pltpu.VMEM((panel_width, half, col_local, span), dtype),
                 pltpu.SemaphoreType.DMA((panel_width,)),
             ],
-            compiler_params=pltpu.CompilerParams(vmem_limit_bytes=32 * 1024 * 1024),
+            compiler_params=pltpu.CompilerParams(vmem_limit_bytes=60 * 1024 * 1024),
         )(orbital_irrep, virtual_panel, vvvv_panel)
 
-    other = lax.ppermute(window(False), "grid", [(g, g ^ 1) for g in range(groups)])
+    swap = [(g, g ^ 1) for g in range(groups)]
+    send_w = window(False)
+    cut = -(-half // 1)
+    other = [lax.ppermute(send_w[i : min(i + cut, half)], "grid", swap) for i in range(0, half, cut)]
+    other = jnp.concatenate(other, axis=0)
     kept = window(True)
 
     row_irrep = orbital_irrep[rep_index * virt_local]

time: 78.5 us -> 78.5 us (level)
  local copies, waits for them, and re-layouts: 8.46 us -> 2.51 us
  Pallas kernels: 5.61 us -> 9.41 us
  waiting for transfers between devices: 21.1 us -> 22.2 us
  matrix products: 1.57 us -> 2.64 us
    unnamed x16 -> x8, local copies, waits for them, and re-layouts: 5.96 us -> 0.03 us
    pallas_call x2, Pallas kernels: 3.44 us -> 7.25 us  [window(): pl.pallas_call(functools.partial(panel_kernel, run, panel_width, own), ou...]
    all_to_all x1, waiting for transfers between devices: 14.9 us -> 17 us  [shards(): lax.all_to_all(sent.reshape(groups, half, pair_local, run), 'grid', 0, 0,...]
    dot_general x2, matrix products: 0.72 us -> 1.79 us  [product(): jnp.einsum('gcjd,cxd->gjx', rows, cols, preferred_element_type=jnp.float32)]
    ppermute x1, waiting for transfers between devices: 6.22 us -> 5.15 us  [shards(): lax.ppermute(send_w[i:min(i + cut, half)], 'grid', swap)]
  transfers between devices with their start and end apart: 2 -> 2, of which waited for: 2 -> 2; matrix products, arithmetic and copies ran while one was open for 6% -> 7% of each run, Pallas kernels for 4% -> 9%
where the time goes in v3:
time: 78.5 us; the launch traced here: 78.1 us
  starting transfers between devices  24.4 us (31%)
  waiting for transfers between devices  22.2 us (28%)
  blocking collectives  15 us (19%)
  Pallas kernels  9.41 us (12%)
  matrix products  2.64 us (3%)
  local copies, waits for them, and re-layouts  2.51 us (3%)
  other arithmetic  1.7 us (2%)
    all_to_all x1, starting transfers between devices, shards(): lax.all_to_all(sent.reshape(groups, half, pair_local, run), 'grid', 0, 0,...  21.2 us
    all_to_all x1, waiting for transfers between devices, shards(): lax.all_to_all(sent.reshape(groups, half, pair_local, run), 'grid', 0, 0,...  17 us
    all_to_all x1, blocking collectives, shards(): lax.all_to_all(outgoing, ('grid', 'rep'), 0, 0, tiled=True, axis_index_gr...  15 us
    pallas_call x2, Pallas kernels, window(): pl.pallas_call(functools.partial(panel_kernel, run, panel_width, own), ou...  7.25 us
    ppermute x1, waiting for transfers between devices, shards(): lax.ppermute(send_w[i:min(i + cut, half)], 'grid', swap)  5.15 us
    ppermute x1, starting transfers between devices, shards(): lax.ppermute(send_w[i:min(i + cut, half)], 'grid', swap)  3.19 us
    pallas_call x1, Pallas kernels, shards(): pl.pallas_call(functools.partial(pack_kernel, run), out_shape=jax.ShapeDt...  2.16 us
    dot_general x2, matrix products, product(): jnp.einsum('gcjd,cxd->gjx', rows, cols, preferred_element_type=jnp.float32)  1.79 us
  transfers between devices with their start and end apart: 2, of which 2 were waited for; matrix products, arithmetic and copies ran while one was open for 7% of the time, Pallas kernels for 9%

profile of v3, /device:TPU:1, one launch (start us, length us, event | category | flops | bytes accessed | tf_op | source)
XLA Modules:
  0.0 78.1 jit_solution(12596059678336065689)
XLA Ops:
  0.0 2.2 %shard_map.64 = bf16[12,2,15,4,240]{4,3,2,1,0:T(4,128)(2,1)} custom-call(s32[960]{0:T(1024)} %orbital_ref.5, s32[96]{0:T(128)} %pair_ref.1, bf16[30,4,960]{2,1,0:T(4,128)(2,1)} %bitcast.40), custom_call_target="tpu_custom_call" | custom-call | tf_op jit(solution)/shard_map/pallas_call | solution.py:84
  2.2 21.2 %all-to-all-start = ((bf16[24,15,4,240]{3,2,1,0:T(4,128)(2,1)}), bf16[24,15,4,240]{3,2,1,0:T(4,128)(2,1)S(1)}, u32[]{:S(2)}, u32[]{:S(2)}) async-start(bf16[24,15,4,240]{3,2,1,0:T(4,128)(2,1)} %bitcast.39), calls=%async_computation | async-start | bytes 1474560 | tf_op jit(solution)/shard_map/all_to_all | solution.py:91
  23.4 3.7 %shard_map.66 = bf16[15,80,240]{2,1,0:T(8,128)(2,1)} custom-call(s32[960]{0:T(1024)} %orbital_ref.5, s32[2]{0:T(128)} %panel_ref.3, bf16[30,40,1920]{2,1,0:T(8,128)(2,1)} %w_ref.3), custom_call_target="tpu_custom_call" | custom-call | tf_op jit(solution)/shard_map/pallas_call | solution.py:94
  27.1 3.2 %collective-permute-start = (bf16[15,80,240]{2,1,0:T(8,128)(2,1)}, bf16[15,80,240]{2,1,0:T(8,128)(2,1)S(1)}, u32[]{:S(2)}, u32[]{:S(2)}) collective-permute-start(bf16[15,80,240]{2,1,0:T(8,128)(2,1)} %shard_map.66), channel_id=1, source_target_pairs={{0,32},{32,0},{64,96},{96,64},{128,160},{160,128},{192,224},{224,1... | collective-permute-start | bytes 1728008 | tf_op jit(solution)/shard_map/ppermute | solution.py:109
  30.3 3.6 %shard_map.65 = bf16[15,80,240]{2,1,0:T(8,128)(2,1)} custom-call(s32[960]{0:T(1024)} %orbital_ref.5, s32[2]{0:T(128)} %panel_ref.3, bf16[30,40,1920]{2,1,0:T(8,128)(2,1)} %w_ref.3), custom_call_target="tpu_custom_call" | custom-call | tf_op jit(solution)/shard_map/pallas_call | solution.py:94
  34.0 0.6 gather_fusion
  34.6 0.6 fusion.20
  35.2 0.6 broadcast_compare_fusion.1
  35.9 0.1 broadcast_select_fusion.2
  35.9 0.1 copy.26
  36.0 0.1 broadcast_in_dim.86
  36.1 0.1 broadcast_in_dim.87
  36.2 0.7 broadcast_xor_fusion
  37.0 0.1 copy.24
  37.3 17.0 %all-to-all-done = bf16[24,15,4,240]{3,2,1,0:T(4,128)(2,1)S(1)} async-done(((bf16[24,15,4,240]{3,2,1,0:T(4,128)(2,1)}), bf16[24,15,4,240]{3,2,1,0:T(4,128)(2,1)S(1)}, u32[]{:S(2)}, u32[]{:S(2)}) %all-to-all-start) | async-done | bytes 691232 | tf_op jit(solution)/shard_map/all_to_all | solution.py:91
  54.3 0.4 convolution_bitcast_fusion.2
  54.8 0.4 convolution_bitcast_fusion
  55.2 1.4 %fusion = f32[24,4,80]{2,0,1:T(8,128)S(1)} fusion(f32[24,4,80]{2,0,1:T(8,128)S(1)} %convolution_bitcast_fusion.2, bf16[15,80,240]{2,1,0:T(8,128)(2,1)} %shard_map.65, bf16[24,15,4,240]{3,2,1,0:T(4,128)(2,1)S(1)} %all-to-all-done), kind=kOutput, calls=%fused_computation.5 | convolution fusion | flops 55303680 | bytes 1328640 | tf_op jit(solution)/shard_map/gcjd,cxd->gjx/dot_general | solution.py:126
  56.6 5.2 %collective-permute-done = bf16[15,80,240]{2,1,0:T(8,128)(2,1)S(1)} collective-permute-done((bf16[15,80,240]{2,1,0:T(8,128)(2,1)}, bf16[15,80,240]{2,1,0:T(8,128)(2,1)S(1)}, u32[]{:S(2)}, u32[]{:S(2)}) %collective-permute-start) | collective-permute-done | bytes 576032 | tf_op jit(solution)/shard_map/ppermute | solution.py:109
  61.8 0.4 broadcast_select_fusion.1
  62.2 0.1 select_n.104
  62.4 15.0 %all_to_all.11 = f32[64,1,240]{2,1,0:T(1,128)S(1)} all-to-all(f32[64,1,240]{2,1,0:T(1,128)S(1)} %select_n.104), channel_id=1, replica_groups={{0,1,2,3,4,5,6,7,8,9,10,11,12,13,14,15,16,17,18,19,20,21,22,23,24,25,26..., dimensions={0} | all-to-all | bytes 122880 | tf_op jit(solution)/shard_map/all_to_all | solution.py:142
  77.3 0.1 reduce_sum.9
  77.4 0.7 reshape.140
  (21 shorter events, 0.3 us)
Async XLA Ops:
  2.2 52.1 %all-to-all-start = ((bf16[24,15,4,240]{3,2,1,0:T(4,128)(2,1)}), bf16[24,15,4,240]{3,2,1,0:T(4,128)(2,1)S(1)}, u32[]{:S(2)}, u32[]{:S(2)}) async-start(bf16[24,15,4,240]{3,2,1,0:T(4,128)(2,1)} %bitcast.39), calls=%async_computation | async-start | bytes 1474560 | tf_op jit(solution)/shard_map/all_to_all | solution.py:91
  23.4 10.6 %copy-start.1 = (s32[2]{0:T(128)S(1)}, s32[2]{0:T(128)}, u32[]{:S(2)}) copy-start(s32[2]{0:T(128)} %panel_ref.3) | copy-start | bytes 28
  23.4 10.6 %copy-start = (s32[960]{0:T(1024)S(1)}, s32[960]{0:T(1024)}, u32[]{:S(2)}) copy-start(s32[960]{0:T(1024)} %orbital_ref.5) | copy-start | bytes 11524
  23.4 12.5 %copy-start.3 = (bf16[30,2]{0,1:T(2,128)(2,1)S(1)}, bf16[30,2]{0,1:T(2,128)(2,1)}, u32[]{:S(2)}) copy-start(bf16[30,2]{0,1:T(2,128)(2,1)} %param.8) | copy-start | bytes 364
  23.4 13.5 %copy-start.2 = (s32[96]{0:T(128)S(1)}, s32[96]{0:T(128)}, u32[]{:S(2)}) copy-start(s32[96]{0:T(128)} %pair_ref.1) | copy-start | bytes 1156
  27.1 34.7 %collective-permute-start = (bf16[15,80,240]{2,1,0:T(8,128)(2,1)}, bf16[15,80,240]{2,1,0:T(8,128)(2,1)S(1)}, u32[]{:S(2)}, u32[]{:S(2)}) collective-permute-start(bf16[15,80,240]{2,1,0:T(8,128)(2,1)} %shard_map.66), channel_id=1, source_target_pairs={{0,32},{32,0},{64,96},{96,64},{128,160},{160,128},{192,224},{224,1... | collective-permute-start | bytes 1728008 | tf_op jit(solution)/shard_map/ppermute | solution.py:109
